TPU v7x, 512 devices: a whole 4x4x16 slice. The times are simulated.
512 devices in a mesh: grp: 8 (over y, core), ep: 64 (over x, z).
Axes of the slice: x: 4, y: 4, z: 16, core: 2. Of those that a mesh axis runs over, the one named last changes fastest.
Arguments:
- tokens: bfloat16 [8192, 4096], P('ep'), may hold values from -6 to 6
- routes: int32 [8192, 8], P('ep'), may hold values from 0 to 127, all different within a row; in each aligned block of 128 rows (0 to 127, 128 to 255, ...) at most 10 rows name the same one
- route_weights: float32 [8192, 8], P('ep'), may hold values from 0.1 to 1
- expert_at_slot: int32 [64], replicated, may hold values from 0 to 127, as said below
- gate_up: bfloat16 [64, 4096, 2, 1024], P('ep', None, None, 'grp')
- down: bfloat16 [64, 1024, 4096], P('ep', 'grp'), may hold values from -0.1875 to 0.1875
Outputs:
- mixed: bfloat16 [8192, 4096], P('ep', 'grp')
- thresholds: float32 [64], replicated
Inputs may be any that keep to these rules, and one draw needn't show every extreme that they name: `routes`: each row names 8 different experts. In the rows of one index of ep no expert is named by more than 10 rows, a bound that some block reaches. `expert_at_slot`: 64 different experts.
All inputs are finite; a program needn't handle non-finite values.
Results may differ from a plain program's by a relative error of at most 0.0057.
Values may be sent and summed in bfloat16 or wider, within the bound.
A program may use at most 64 MiB of HBM per device.

v0:
```python
import math

import jax
import jax.numpy as jnp
from jax import lax
from jax.sharding import PartitionSpec as P

NB = 128
CAP = 10


hist_top = 16.0
quantile = 0.999


def soft_counts(values, row_weight, bin_count):
    width_bin = hist_top / bin_count
    magnitude = jnp.abs(values.astype(jnp.float32)).reshape(-1)
    weight_flat = jnp.broadcast_to(row_weight[:, None], values.shape).reshape(-1)
    block_size = math.gcd(magnitude.shape[0], 8192)
    centers = jnp.arange(bin_count, dtype=jnp.float32)

    def one_block(packed):
        levels, shares = packed
        position = jnp.clip(levels / width_bin - 0.5, 0.0, bin_count - 1.0)
        lower = jnp.floor(position)
        upper_share = position - lower
        table = (lower[:, None] == centers[None, :]).astype(jnp.bfloat16)
        paired = jnp.stack([shares * (1.0 - upper_share), shares * upper_share])
        return jnp.dot(
            paired, table, preferred_element_type=jnp.float32, precision=lax.Precision.HIGHEST
        )

    partials = lax.map(
        one_block, (magnitude.reshape(-1, block_size), weight_flat.reshape(-1, block_size))
    )
    summed = jnp.sum(partials, axis=0)
    raised = jnp.concatenate([jnp.zeros((1,), jnp.float32), summed[1, :-1]])
    return summed[0] + raised


def clip_from(counts, bin_count):
    width_bin = hist_top / bin_count
    totals = jnp.sum(counts, axis=-1, keepdims=True)
    before = jnp.cumsum(counts, axis=-1) - counts
    fraction = jnp.clip((quantile * totals - before) / jnp.maximum(counts, 1.0), 0.0, 1.0)
    return width_bin * jnp.sum(fraction, axis=-1)


def per_device(tokens, routes, route_weights, expert_at_slot, gate_up, down):
    slot_count = expert_at_slot.shape[0]
    token_count, pick_count = routes.shape
    model_width = tokens.shape[1]
    capacity = CAP
    buffer_rows = slot_count * capacity
    ep_index = lax.axis_index("ep")
    gate_up_local = gate_up[0]
    down_local = down[0]
    slice_hidden = down_local.shape[0]
    matches = routes[:, :, None] == expert_at_slot[None, None, :]
    in_flight = jnp.any(matches, axis=2)
    slot_ids = jnp.sum(jnp.where(matches, jnp.arange(slot_count, dtype=jnp.int32), 0), axis=2)
    onehot_slots = matches.reshape(token_count * pick_count, slot_count).astype(jnp.int32)
    earlier_count = jnp.cumsum(onehot_slots, axis=0) - onehot_slots
    position = jnp.sum(earlier_count * onehot_slots, axis=1).reshape(token_count, pick_count)
    target = slot_ids * capacity + position
    placing = (
        target.reshape(-1)[:, None] == jnp.arange(buffer_rows, dtype=jnp.int32)[None, :]
    ) & in_flight.reshape(-1)[:, None]
    token_ids = jnp.repeat(jnp.arange(token_count, dtype=jnp.int32), pick_count)
    source_row = jnp.sum(jnp.where(placing, token_ids[:, None], 0), axis=0)
    occupied = jnp.any(placing, axis=0)
    send_rows = jnp.where(
        occupied[:, None], tokens[source_row], jnp.zeros((), tokens.dtype)
    ).reshape(slot_count, capacity, model_width)
    send_mask = occupied.astype(jnp.bfloat16).reshape(slot_count, capacity)
    rows_in = lax.all_to_all(send_rows, "ep", split_axis=0, concat_axis=0, tiled=True)
    mask_in = lax.all_to_all(send_mask, "ep", split_axis=0, concat_axis=0, tiled=True)
    gate_and_up = jnp.einsum(
        "scd,dgh->scgh", rows_in, gate_up_local, preferred_element_type=jnp.float32
    )
    hidden_rows = (jax.nn.silu(gate_and_up[:, :, 0, :]) * gate_and_up[:, :, 1, :]).astype(
        jnp.bfloat16
    )
    output_rows = jnp.einsum(
        "sch,hd->scd", hidden_rows, down_local, preferred_element_type=jnp.float32
    ).astype(jnp.bfloat16)
    output_rows, hidden_rows = (output_rows, hidden_rows)
    counts_local = soft_counts(
        hidden_rows.reshape(-1, slice_hidden), mask_in.reshape(-1).astype(jnp.float32), NB
    )
    counts_slot = lax.psum(counts_local, "grp")
    clip_own = clip_from(counts_slot, NB)
    placed = jnp.where(jnp.arange(slot_count, dtype=jnp.int32) == ep_index, clip_own, 0.0)
    thresholds = lax.psum(placed, "ep")
    safe_target = jnp.where(in_flight, target, 0)
    weights_used = jnp.where(in_flight, route_weights, 0.0)
    returned = lax.all_to_all(output_rows, "ep", split_axis=0, concat_axis=0, tiled=True)
    flat_back = returned.reshape(buffer_rows, model_width)
    picked_rows = flat_back[safe_target]
    combined = jnp.sum(weights_used[:, :, None] * picked_rows.astype(jnp.float32), axis=1)
    mixed_share = lax.psum_scatter(combined, "grp", scatter_dimension=1, tiled=True)
    return (mixed_share.astype(jnp.bfloat16), thresholds)


def solution(mesh):
    placed = (
        P("ep", None),
        P("ep", None),
        P("ep", None),
        P(),
        P("ep", None, None, "grp"),
        P("ep", "grp", None),
    )
    return jax.shard_map(
        per_device, mesh=mesh, in_specs=placed, out_specs=(P("ep", "grp"), P()), check_vma=False
    )
```

profile of v0, /device:TPU:32, one launch (start us, length us, event | category | flops | bytes accessed | tf_op | source)
XLA Modules:
  0.0 1069.4 jit_solution(6624361917194619826)
XLA Ops:
  7.2 0.9 copy.40
  8.2 0.8 fusion.19
  9.0 0.8 compare_reduce_fusion
  9.8 0.8 compare_convert_fusion.1
  10.6 18.0 %reduce-window.19 = s32[64,8,128]{2,1,0:T(8,128)S(1)} reduce-window(s32[64,8,128]{2,1,0:T(8,128)S(1)} %compare_convert_fusion.1, s32[]{:T(128)} %copy.74), window={size=1x1x128 pad=0_0x0_0x127_0}, to_apply=%region_2.3 | reduce-window | flops 8323072 | bytes 524292 | tf_op jit(solution)/shard_map/reduce-window
  28.8 0.1 copy.42
  29.6 0.8 fusion.21
  30.4 0.8 fusion.15
  31.2 0.1 broadcast_in_dim.86
  31.5 0.8 select_reduce_fusion
  32.4 5.4 gather_fusion
  37.7 8.2 gather.9
  46.0 7.2 broadcast_select_fusion
  53.2 18.4 %all-to-all-start = ((bf16[64,10,4096]{2,1,0:T(8,128)(2,1)}), bf16[64,10,4096]{2,1,0:T(8,128)(2,1)}, u32[]{:S(2)}, u32[]{:S(2)}) async-start(bf16[64,10,4096]{2,1,0:T(8,128)(2,1)} %broadcast_select_fusion), calls=%async_computation | async-start | bytes 16777216 | tf_op jit(solution)/shard_map/all_to_all | solution.py:77
  71.6 0.8 reshape.211
  72.4 367.3 %all-to-all-done = bf16[64,10,4096]{2,1,0:T(8,128)(2,1)} async-done(((bf16[64,10,4096]{2,1,0:T(8,128)(2,1)}), bf16[64,10,4096]{2,1,0:T(8,128)(2,1)}, u32[]{:S(2)}, u32[]{:S(2)}) %all-to-all-start) | async-done | bytes 5242912 | tf_op jit(solution)/shard_map/all_to_all | solution.py:77
  439.6 7.2 all-to-all-start.2
  446.9 9.7 fusion.12
  456.6 1.5 convolution_convert_fusion
  458.2 6.4 copy.47
  464.6 15.5 %all-to-all-start.1 = ((bf16[64,10,4096]{2,1,0:T(8,128)(2,1)}), bf16[64,10,4096]{2,1,0:T(8,128)(2,1)}, u32[]{:S(2)}, u32[]{:S(2)}) async-start(bf16[64,10,4096]{2,1,0:T(8,128)(2,1)} %copy.47), calls=%async_computation.1 | async-start | bytes 16777216 | tf_op jit(solution)/shard_map/all_to_all | solution.py:98
  480.0 0.3 reduce-scatter.2.cloned.1.call-start
  481.0 0.1 broadcast_in_dim.95
  481.2 0.3 copy.58
  481.6 0.2 copy.51
  481.9 0.2 copy.52
  482.2 0.1 convert_abs_fusion
  482.4 363.9 %all-to-all-done.1 = bf16[64,10,4096]{2,1,0:T(8,128)(2,1)} async-done(((bf16[64,10,4096]{2,1,0:T(8,128)(2,1)}), bf16[64,10,4096]{2,1,0:T(8,128)(2,1)}, u32[]{:S(2)}, u32[]{:S(2)}) %all-to-all-start.1) | async-done | bytes 5242912 | tf_op jit(solution)/shard_map/all_to_all | solution.py:98
  846.3 8.6 reshape.184
  854.9 18.2 %gather_fusion.1 = bf16[1024,4096]{1,0:T(8,128)(2,1)} fusion(bf16[640,4096]{1,0:T(8,128)(2,1)} %reshape.184, s32[1024]{0:T(1024)S(1)} %broadcast_clamp_fusion), kind=kCustom, calls=%fused_computation.1 | custom fusion | bytes 16781312 | tf_op jit(solution)/shard_map/gather | solution.py:100
  873.1 13.2 %fusion.11 = f32[128,4096]{1,0:T(8,128)} fusion(bf16[1024,4096]{1,0:T(8,128)(2,1)} %gather_fusion.1, f32[128,8]{1,0:T(8,128)S(1)} %copy.38), kind=kLoop, calls=%fused_computation.17 | loop fusion | flops 12058624 | bytes 10489856 | tf_op jit(solution)/shard_map/reduce_sum | solution.py:101
  886.3 19.4 %while.13 = (s32[]{:T(128)}, f32[10,2,128]{2,1,0:T(2,128)S(1)}, f32[10,8192]{1,0:T(8,128)S(1)}, f32[10,8192]{1,0:T(8,128)S(1)}, s32[]{:T(128)}) while((s32[]{:T(128)}, f32[10,2,128]{2,1,0:T(2,128)S(1)}, f32[10,8192]{1,0:T(8,128)S(1)}, f32[10,8192]{1,0:T(8,128)S(1)}, s32[]{:T(128)}) %tuple.43), condition=%wide.region_10.11_spmd.clone, body=%wide.region_9.10_spmd.clone.sunk | while | flops 26296320 | bytes 263237 | solution.py:34
  886.5 1.8 fusion.32
  888.4 1.8 fusion.32
  890.4 1.8 fusion.32
  892.3 1.8 fusion.32
  894.2 1.8 fusion.32
  896.2 1.8 fusion.32
  898.1 1.8 fusion.32
  900.1 1.8 fusion.32
  902.0 1.8 fusion.32
  903.9 1.8 fusion.32
  905.9 12.4 %psum.14 = f32[128]{0:T(128)S(1)} all-reduce(f32[128]{0:T(128)S(1)} %maximum_add_fusion), channel_id=1, replica_groups=mesh['grp'=8,'ep'=64] {'grp'}, use_global_device_ids=true, to_apply=%region_12.13 | all-reduce | flops 128 | bytes 1024 | tf_op jit(solution)/shard_map/psum | solution.py:92
  918.3 0.6 reduce_sum.71
  919.0 0.2 reduce-window.21
  919.9 0.6 clamp_reduce_fusion
  921.2 139.7 %psum.15 = f32[64]{0:T(128)} all-reduce(f32[64]{0:T(128)S(1)} %compare_select_fusion.4), channel_id=1, replica_groups=mesh['grp'=8,'ep'=64] {'ep'}, use_global_device_ids=true, to_apply=%region_16.17 | all-reduce | flops 64 | bytes 512 | tf_op jit(solution)/shard_map/psum | solution.py:95
  1060.9 1.6 convert_element_type.61
  (60 shorter events, 3.6 us)
Async XLA Ops:
  7.2 25.2 %copy-start = (bf16[128,4096]{1,0:T(8,128)(2,1)S(1)}, bf16[128,4096]{1,0:T(8,128)(2,1)}, u32[]{:S(2)}) copy-start(bf16[128,4096]{1,0:T(8,128)(2,1)} %param.8) | copy-start | bytes 3145732
  53.2 386.5 %all-to-all-start = ((bf16[64,10,4096]{2,1,0:T(8,128)(2,1)}), bf16[64,10,4096]{2,1,0:T(8,128)(2,1)}, u32[]{:S(2)}, u32[]{:S(2)}) async-start(bf16[64,10,4096]{2,1,0:T(8,128)(2,1)} %broadcast_select_fusion), calls=%async_computation | async-start | bytes 16777216 | tf_op jit(solution)/shard_map/all_to_all | solution.py:77
  439.6 24.9 %all-to-all-start.2 = ((bf16[64,1,10]{2,1,0:T(2,128)(2,1)}), bf16[64,1,10]{2,1,0:T(2,128)(2,1)S(1)}, u32[]{:S(2)}, u32[]{:S(2)}) async-start(bf16[64,1,10]{2,1,0:T(2,128)(2,1)} %reshape.211), calls=%async_computation.3 | async-start | bytes 65536 | tf_op jit(solution)/shard_map/all_to_all | solution.py:78
  446.9 9.7 copy-start.2
  464.6 16.1 %copy-start.3 = (f32[128,8]{0,1:T(8,128)S(1)}, f32[128,8]{0,1:T(8,128)}, u32[]{:S(2)}) copy-start(f32[128,8]{0,1:T(8,128)} %param.10) | copy-start | bytes 12292
  464.6 381.7 %all-to-all-start.1 = ((bf16[64,10,4096]{2,1,0:T(8,128)(2,1)}), bf16[64,10,4096]{2,1,0:T(8,128)(2,1)}, u32[]{:S(2)}, u32[]{:S(2)}) async-start(bf16[64,10,4096]{2,1,0:T(8,128)(2,1)} %copy.47), calls=%async_computation.1 | async-start | bytes 16777216 | tf_op jit(solution)/shard_map/all_to_all | solution.py:98
  480.0 580.9 %reduce-scatter.2.cloned.1.call-start = ((), (), s32[]{:S(2)}) async-start(), calls=%async_computation.4 | async-start | bytes 2359296 | tf_op jit(solution)/shard_map/reduce_scatter | solution.py:102
  886.3 176.2 %copy-start.1 = (bf16[128,4096]{1,0:T(8,128)(2,1)S(1)}, bf16[128,4096]{1,0:T(8,128)(2,1)}, u32[]{:S(2)}) copy-start(bf16[128,4096]{1,0:T(8,128)(2,1)} %param.8) | copy-start | bytes 3145732
Sparse Core Ops, SparseCore 0:
  886.5 34.9 reduce-scatter.1
where the time goes:
time: 1070 us
  waiting for transfers between devices  731 us (68%)
  blocking collectives  152 us (14%)
  local copies, waits for them, and re-layouts  51.5 us (5%)
  other arithmetic  48.1 us (4%)
  starting transfers between devices  41.3 us (4%)
  matrix products  29.2 us (3%)
  between operations  15.7 us (1%)
    all_to_all x1, waiting for transfers between devices, per_device(): lax.all_to_all(send_rows, 'ep', split_axis=0, concat_axis=0, tiled=True)  367 us
    all_to_all x1, waiting for transfers between devices, per_device(): lax.all_to_all(output_rows, 'ep', split_axis=0, concat_axis=0, tiled=True)  364 us
    psum x1, blocking collectives, per_device(): thresholds = lax.psum(placed, 'ep')  140 us
  transfers between devices with their start and end apart: 4, of which 2 were waited for; matrix products, arithmetic and copies ran while one was open for 4% of the time, Pallas kernels for 0%

commit v1 on v0

v1 whole, which is shorter than its diff:
```python
import functools

import jax
import jax.numpy as jnp
import numpy as np
from jax import lax
from jax.experimental import pallas as pl
from jax.experimental.pallas import tpu as pltpu
from jax.sharding import PartitionSpec as P

NB = 128
CAP = 10
NY = 4
NC = 2
NX = 4
NZ = 16
HIST_TOP = 16.0
QUANTILE = 0.999
MESH = pl.DeviceIdType.MESH
F32 = jnp.float32
BF16 = jnp.bfloat16
HIGHEST = lax.Precision.HIGHEST
SEMS = 160


def dot(a, b, precision=None):
    return jnp.dot(a, b, preferred_element_type=F32, precision=precision)


def dot_nt(a, b):
    return lax.dot_general(a, b, (((1,), (1,)), ((), ())), preferred_element_type=F32)


def mask_bf16(m):
    return jnp.where(m, 1.0, 0.0).astype(BF16)


def iota(shape, dim):
    return lax.broadcasted_iota(jnp.int32, shape, dim)


def kernel(
    nx,
    nz,
    tokens,
    routes,
    route_weights,
    slots,
    gate_up,
    down,
    lane_info,
    perm_info,
    mixed,
    thresholds,
    tokz,
    meta,
    xsend,
    rows,
    w_raw,
    w_split,
    dn,
    acc,
    hid,
    outs,
    outr,
    zsend,
    zrecv,
    weights_hi,
    weights_lo,
    total,
    hist,
    valid_send,
    valid_recv,
    count_recv,
    th_send,
    th_recv,
    tx_send,
    tx_recv,
    send_sems,
    recv_sems,
    local_sems,
):
    ng = NY * NC
    per_group = nz // 2
    block_rows = per_group * CAP
    group_rows = nx * block_rows
    t_count = tokens.shape[0]
    feat = tokens.shape[1] // ng
    half_t = t_count // 2
    h_local = down.shape[0]

    g = lax.axis_index("grp")
    ep = lax.axis_index("ep")
    y, c = lax.div(g, NC), lax.rem(g, NC)
    x, z = lax.div(ep, nz), lax.rem(ep, nz)
    y_up, y_dn, y_op = lax.rem(y + 1, NY), lax.rem(y + NY - 1, NY), lax.rem(y + 2, NY)
    other = 1 - c
    z_up, z_dn = lax.rem(z + 1, nz), lax.rem(z + nz - 1, nz)

    def sl(j):
        return (j + nz // 4) % nz

    def at_z(zz):
        return (g, x * nz + zz)

    def at_x(xx):
        return (g, xx * nz + z)

    def at_g(gg):
        return (gg, ep)

    def g_of(yy, cc):
        return yy * NC + cc

    started = []
    used = [0]

    def send(src, dst, device):
        k = used[0]
        used[0] += 1
        copy = pltpu.make_async_remote_copy(
            src_ref=src,
            dst_ref=dst,
            send_sem=send_sems.at[k],
            recv_sem=recv_sems.at[k],
            device_id=device,
            device_id_type=MESH,
        )
        copy.start()
        started.append(copy)
        return k

    def arrived(k, ref):
        pltpu.make_async_remote_copy(
            src_ref=ref,
            dst_ref=ref,
            send_sem=send_sems.at[k],
            recv_sem=recv_sems.at[k],
            device_id=(g, ep),
            device_id_type=MESH,
        ).wait_recv()

    own = sl(0)
    take_tokens = pltpu.make_async_copy(
        tokens.at[:, pl.ds(pl.multiple_of(g * feat, 128), feat)], tokz.at[own], local_sems.at[0]
    )
    take_tokens.start()
    take_w = pltpu.make_async_copy(gate_up, w_raw, local_sems.at[1])
    take_w.start()
    take_down = pltpu.make_async_copy(
        down.at[:, pl.ds(pl.multiple_of(g * feat, 128), feat)], dn.at[g], local_sems.at[2]
    )
    take_down.start()

    barrier = pltpu.get_barrier_semaphore()
    peers = 0
    for j in range(1, nz):
        pl.semaphore_signal(barrier, inc=1, device_id=at_z(lax.rem(z + j, nz)), device_id_type=MESH)
        peers += 1
    for i in range(1, nx):
        pl.semaphore_signal(barrier, inc=1, device_id=at_x(lax.rem(x + i, nx)), device_id_type=MESH)
        peers += 1
    for q in range(1, ng):
        pl.semaphore_signal(barrier, inc=1, device_id=at_g(lax.rem(g + q, ng)), device_id_type=MESH)
        peers += 1

    picks = routes.shape[1]
    routes_f = routes[...].astype(F32).astype(BF16)
    spread = mask_bf16(iota((16, picks), 0) == iota((16, picks), 1))
    meta[own] = dot_nt(spread, routes_f).astype(BF16)

    pl.semaphore_wait(barrier, peers)
    take_tokens.wait()

    ring = {}

    def ring_send(s):
        for h in range(2):
            part = pl.ds(h * half_t, half_t)
            if s < nz // 2 or h == 0:
                ring["up", s, h] = send(
                    tokz.at[sl(s - 1), part], tokz.at[sl(s), part], at_z(z_up)
                )
            if s < nz // 2 or h == 1:
                ring["dn", s, h] = send(
                    tokz.at[sl(1 - s), part], tokz.at[sl(-s), part], at_z(z_dn)
                )
            if h == 0:
                ring["up", s] = send(meta.at[sl(s - 1)], meta.at[sl(s)], at_z(z_up))
                if s < nz // 2:
                    ring["dn", s] = send(meta.at[sl(1 - s)], meta.at[sl(-s)], at_z(z_dn))

    def ring_wait(s):
        for h in range(2):
            part = pl.ds(h * half_t, half_t)
            if s < nz // 2 or h == 0:
                arrived(ring["up", s, h], tokz.at[sl(s), part])
            if s < nz // 2 or h == 1:
                arrived(ring["dn", s, h], tokz.at[sl(-s), part])
        arrived(ring["up", s], meta.at[sl(s)])
        if s < nz // 2:
            arrived(ring["dn", s], meta.at[sl(-s)])

    tri = mask_bf16(iota((t_count, t_count), 0) < iota((t_count, t_count), 1))
    experts_here = jnp.full((8, 1), -1.0, F32)
    for i in range(nx):
        e = slots[lax.rem(x + i, nx) * nz + z].astype(F32)
        experts_here = jnp.where(iota((8, 1), 0) == i, e, experts_here)

    valid_sum = [jnp.zeros((8, t_count), F32)]
    x_keys = {}

    def select(grp_no):
        chosen = []
        for s in range(grp_no * per_group, (grp_no + 1) * per_group):
            table = meta[s].astype(F32)
            hit = jnp.zeros((8, t_count), F32)
            for k in range(picks):
                hit = jnp.maximum(hit, jnp.where(table[k : k + 1, :] == experts_here, 1.0, 0.0))
            valid_sum[0] = valid_sum[0] + hit
            chosen.append(hit)
        stacked = jnp.concatenate(chosen, axis=0)
        earlier = dot(stacked.astype(BF16), tri)
        first = lax.shift_right_logical(iota((8 * per_group, t_count), 0), 3) * CAP
        code = jnp.where(stacked > 0.5, earlier + first.astype(F32), -1.0)
        row = iota((block_rows, t_count), 0).astype(F32)
        values = tokz[grp_no * per_group : (grp_no + 1) * per_group].reshape(
            per_group * t_count, feat
        )
        for i in range(nx):
            sel = jnp.concatenate(
                [mask_bf16(row == code[8 * s + i : 8 * s + i + 1, :]) for s in range(per_group)],
                axis=1,
            )
            picked = dot(sel, values).astype(BF16)
            if i == 0:
                rows[g, grp_no, 0] = picked
            else:
                xsend[grp_no, i - 1] = picked
                x_keys[grp_no, i] = send(
                    xsend.at[grp_no, i - 1], rows.at[g, grp_no, i], at_x(lax.rem(x + i, nx))
                )

    def broadcast(ref):
        up, dn_, op = g_of(y_up, c), g_of(y_dn, c), g_of(y_op, c)
        mate = at_g(g_of(y, other))
        a_up = send(ref(g), ref(g), at_g(up))
        a_dn = send(ref(g), ref(g), at_g(dn_))
        a_mate = send(ref(g), ref(g), mate)
        yield
        arrived(a_up, ref(dn_))
        b_up = send(ref(dn_, 0), ref(dn_, 0), at_g(up))
        b_mate0 = send(ref(dn_), ref(dn_), mate)
        arrived(a_dn, ref(up))
        b_dn = send(ref(up, 1), ref(up, 1), at_g(dn_))
        b_mate1 = send(ref(up), ref(up), mate)
        yield
        arrived(b_up, ref(op, 0))
        c_mate0 = send(ref(op, 0), ref(op, 0), mate)
        arrived(b_dn, ref(op, 1))
        c_mate1 = send(ref(op, 1), ref(op, 1), mate)
        yield
        arrived(a_mate, ref(g_of(y, other)))
        arrived(b_mate0, ref(g_of(y_dn, other)))
        arrived(b_mate1, ref(g_of(y_up, other)))
        arrived(c_mate0, ref(g_of(y_op, other), 0))
        arrived(c_mate1, ref(g_of(y_op, other), 1))
        yield

    def rows_part(grp_no):
        def ref(q, half=None):
            if half is None:
                return rows.at[q, grp_no]
            return rows.at[q, grp_no, pl.ds(half * (nx // 2), nx // 2)]

        return ref

    def hid_part(grp_no):
        def ref(q, half=None):
            if half is None:
                return hid.at[q, grp_no]
            return hid.at[q, grp_no, pl.ds(half * (group_rows // 2), group_rows // 2)]

        return ref

    def x_arrived(grp_no):
        for i in range(1, nx):
            arrived(x_keys[grp_no, i], rows.at[g, grp_no, i])

    def gate_and_up(grp_no):
        acc[...] = jnp.zeros_like(acc)

        @pl.loop(0, ng)
        def _(q):
            block = rows[q, grp_no].reshape(group_rows, feat)
            acc[...] += dot(block, w_split[q])

        gate = acc[:, :h_local]
        hidden = gate / (1.0 + jnp.exp(-gate)) * acc[:, h_local:]
        hid[g, grp_no] = hidden.astype(BF16)

    def histogram(grp_no):
        wide = 16

        @pl.loop(0, group_rows // wide)
        def _(step):
            first = pl.multiple_of(step * wide, wide)
            level = jnp.abs(hid[g, grp_no, pl.ds(first, wide)].astype(F32))
            where = jnp.clip(level * (NB / HIST_TOP) - 0.5, 0.0, NB - 1.0)
            lower = jnp.floor(where)
            part = where - lower
            part_hi = part.astype(BF16).astype(F32)
            part_lo = part - part_hi
            coarse = jnp.floor(lower * (1.0 / 16.0))
            fine = lower - 16.0 * coarse
            eight = iota((8, h_local), 0).astype(F32)
            sixteen = iota((16, h_local), 0).astype(F32)
            left, one, high, low = [], [], [], []
            for r in range(wide):
                left.append(jnp.where(coarse[r : r + 1] == eight, 1.0, 0.0))
                match = fine[r : r + 1] == sixteen
                one.append(jnp.where(match, 1.0, 0.0))
                high.append(jnp.where(match, part_hi[r : r + 1], 0.0))
                low.append(jnp.where(match, part_lo[r : r + 1], 0.0))
            a = jnp.concatenate(left, axis=0).astype(BF16)
            b = jnp.concatenate(one + high + low, axis=0).astype(BF16)
            hist[...] += dot_nt(a, b)

    def counts_of():
        own_row = lax.shift_right_logical(iota((128, 256), 0), 3) == lax.shift_right_logical(
            iota((128, 256), 1), 4
        )
        fold = jnp.where((iota((256, NB), 0) & 15) == (iota((256, NB), 1) & 15), 1.0, 0.0)
        own_bin = (iota((128, NB), 0) & 7) == lax.shift_right_logical(iota((128, NB), 1), 4)

        def bins(table):
            folded = dot(jnp.where(own_row, table, 0.0), fold, HIGHEST)
            return jnp.sum(jnp.where(own_bin, folded, 0.0), axis=0, keepdims=True)

        number = bins(hist[:, :256])
        share = bins(hist[:, 256:512] + hist[:, 512:])
        share8 = jnp.broadcast_to(share, (8, NB))
        return jnp.broadcast_to(number, (8, NB)) - share8 + pltpu.roll(share8, 1, 1)

    def output_rows(grp_no):
        @pl.loop(0, nx)
        def _(i):
            first = pl.multiple_of(i * block_rows, 16)
            full_i = jnp.concatenate(
                [hid[q, grp_no, pl.ds(first, block_rows)] for q in range(ng)], axis=1
            )
            outs[grp_no, i] = dot(full_i, dn[...].reshape(ng * h_local, feat)).astype(BF16)

    o_keys = {}

    def x_return(grp_no):
        for i in range(1, nx):
            o_keys[grp_no, i] = send(
                outs.at[grp_no, i], outr.at[grp_no, i], at_x(lax.rem(x + nx - i, nx))
            )
        outr[grp_no, 0] = outs[grp_no, 0]

    z_keys = {}
    back_rows = 2 * nx * CAP
    half_f = feat // 2

    def z_return(grp_no):
        for i in range(1, nx):
            arrived(o_keys[grp_no, i], outr.at[grp_no, i])
        col = iota((back_rows, group_rows), 1)
        both = outr[grp_no].reshape(group_rows, feat)
        for k in range(per_group):
            s = grp_no * per_group + k
            upper = mask_bf16(col == perm_info[:, 0:1] + k * CAP)
            under = mask_bf16(col == perm_info[:, 1:2] + k * CAP)
            packed = (dot(upper, both[:, :half_f]) + dot(under, both[:, half_f:])).astype(BF16)
            j = (s - nz // 4) % nz
            if j == 0:
                zrecv[s] = packed
            else:
                zsend[s] = packed
                z_keys[s] = send(zsend.at[s], zrecv.at[s], at_z(lax.rem(z + nz - j, nz)))

    lanes = nz * back_rows

    def home_weights():
        chunk = 128
        index = lane_info[0:1, :]
        expert = jnp.full((1, lanes), -1, jnp.int32)
        for s in range(nz):
            j = (s - nz // 4) % nz
            for i in range(nx):
                e = slots[lax.rem(x + i, nx) * nz + lax.rem(z + j, nz)]
                expert = jnp.where(index == s * nx + i, e, expert)
        before = mask_bf16(iota((t_count, t_count), 1) < iota((t_count, t_count), 0))
        for q in range(0, lanes, chunk):
            part = slice(q, min(q + chunk, lanes))
            e = expert[:, part]
            hit = jnp.zeros((t_count, e.shape[1]), F32)
            weight = hit
            for k in range(picks):
                eq = routes[:, k : k + 1] == e
                hit = jnp.where(eq, 1.0, hit)
                weight = jnp.where(eq, route_weights[:, k : k + 1], weight)
            earlier = dot(before, hit.astype(BF16))
            place = lane_info[1:2, part].astype(F32)
            used_weight = jnp.where((hit > 0.5) & (earlier == place), weight, 0.0)
            top = used_weight.astype(BF16)
            weights_hi[:, part] = top
            weights_lo[:, part] = (used_weight - top.astype(F32)).astype(BF16)

    def combine(grp_no):
        width = per_group * back_rows
        part = slice(grp_no * width, (grp_no + 1) * width)
        back = zrecv[grp_no * per_group : (grp_no + 1) * per_group].reshape(width, half_f)
        for half in range(2):
            keep = lane_info[2:3, part] == half
            zero = jnp.zeros((), BF16)
            high = jnp.where(keep, weights_hi[:, part], zero)
            low = jnp.where(keep, weights_lo[:, part], zero)
            gained = dot(high, back) + dot(low, back)
            cols = slice(half * half_f, (half + 1) * half_f)
            if grp_no == 0:
                total[:, cols] = gained
            else:
                mixed[:, cols] = (total[:, cols] + gained).astype(BF16)

    def wait_back(grp_no):
        for k in range(per_group):
            s = grp_no * per_group + k
            if s in z_keys:
                arrived(z_keys[s], zrecv.at[s])

    def split_weights():
        take_w.wait()
        size = 2 * 128
        r, q = iota((size, size), 0), iota((size, size), 1)
        source = jnp.where(r < 128, 2 * r, 2 * (r - 128) + 1)
        order = mask_bf16(q == source)
        per = feat // 128

        @pl.loop(0, ng)
        def _(gg):
            for b in range(per):
                first = pl.multiple_of((gg * per + b) * size, size)
                mixed_up = dot(order, w_raw[pl.ds(first, size)]).astype(BF16)
                w_split[gg, b * 128 : (b + 1) * 128, :h_local] = mixed_up[:128]
                w_split[gg, b * 128 : (b + 1) * 128, h_local:] = mixed_up[128:]

    down_keys = []

    def send_down():
        for q in range(1, ng):
            to = lax.rem(g + q, ng)
            columns = pl.ds(pl.multiple_of(to * feat, 128), feat)
            down_keys.append(send(down.at[:, columns], dn.at[g], at_g(to)))

    rows_a, rows_b = None, None

    ring_send(1)
    send_down()
    hist[...] = jnp.zeros_like(hist)
    split_weights()
    bcast = {}

    def start_rows(grp_no):
        x_arrived(grp_no)
        bcast[grp_no] = broadcast(rows_part(grp_no))
        next(bcast[grp_no])

    stages = [
        lambda: select(0),
        lambda: start_rows(0),
        lambda: next(bcast[0]),
        lambda: next(bcast[0]),
    ]
    for s in range(2, nz // 2 + 1):
        ring_wait(s - 1)
        ring_send(s)
        if s == 2:
            home_weights()
        if s > nz // 4 and stages:
            stages.pop(0)()
    ring_wait(nz // 2)
    select(1)
    for stage in stages:
        stage()

    number = jnp.broadcast_to(jnp.sum(valid_sum[0], axis=1, keepdims=True), (8, 128))
    valid_keys = {}
    for i in range(nx):
        line = jnp.broadcast_to(number[i : i + 1, :], (8, 128))
        if i == 0:
            valid_recv[0] = line
        else:
            valid_send[i - 1] = line
            valid_keys[i] = send(
                valid_send.at[i - 1], valid_recv.at[i], at_x(lax.rem(x + i, nx))
            )

    next(bcast[0])
    gate_and_up(0)
    hidden_a = broadcast(hid_part(0))
    next(hidden_a)
    start_rows(1)
    next(hidden_a)
    next(bcast[1])
    histogram(0)
    next(hidden_a)
    take_down.wait()
    for q in range(1, ng):
        arrived(down_keys[q - 1], dn.at[lax.rem(g + ng - q, ng)])
    next(hidden_a)
    output_rows(0)
    x_return(0)
    next(bcast[1])
    next(bcast[1])
    gate_and_up(1)
    hidden_b = broadcast(hid_part(1))
    next(hidden_b)
    z_return(0)
    next(hidden_b)
    histogram(1)
    counts = counts_of()
    filled = valid_recv[0]
    for i in range(1, nx):
        arrived(valid_keys[i], valid_recv.at[i])
        filled = filled + valid_recv[i]
    empty = (float(2 * group_rows) - filled) * float(h_local)
    counts = counts - jnp.where(iota((8, NB), 1) == 0, empty, 0.0)
    count_recv[g] = counts
    count_keys = {}
    for q in range(1, ng):
        count_keys[q] = send(count_recv.at[g], count_recv.at[g], at_g(lax.rem(g + q, ng)))
    next(hidden_b)
    next(hidden_b)
    output_rows(1)
    x_return(1)

    for q in range(1, ng):
        from_g = lax.rem(g + ng - q, ng)
        arrived(count_keys[q], count_recv.at[from_g])
    counts = count_recv[0]
    for q in range(1, ng):
        counts = counts + count_recv[q]
    sums = jnp.sum(counts, axis=1, keepdims=True)
    below = jnp.where(iota((NB, NB), 0) < iota((NB, NB), 1), 1.0, 0.0)
    before_bin = dot(counts, below, HIGHEST)
    fraction = jnp.clip((QUANTILE * sums - before_bin) / jnp.maximum(counts, 1.0), 0.0, 1.0)
    threshold = (HIST_TOP / NB) * jnp.sum(fraction, axis=1, keepdims=True)
    th_send[...] = jnp.broadcast_to(threshold, (8, 128))
    th_recv[0] = th_send[...]
    th_keys = {}
    for j in range(1, nz):
        th_keys[j] = send(th_send, th_recv.at[j], at_z(lax.rem(z + j, nz)))
    z_return(1)
    gathered = jnp.zeros((8, 128), F32)
    for j in range(nz):
        if j:
            arrived(th_keys[j], th_recv.at[j])
        place = x * nz + lax.rem(z + nz - j, nz)
        gathered = jnp.where(iota((8, 128), 1) == place, th_recv[j], gathered)
    tx_send[...] = gathered
    tx_keys = {}
    for i in range(1, nx):
        tx_keys[i] = send(tx_send, tx_recv.at[i - 1], at_x(lax.rem(x + i, nx)))

    wait_back(0)
    combine(0)
    for i in range(1, nx):
        arrived(tx_keys[i], tx_recv.at[i - 1])
        gathered = gathered + tx_recv[i - 1]
    thresholds[...] = gathered
    wait_back(1)
    combine(1)
    for copy in started:
        copy.wait_send()


def per_device(nx, nz, tokens, routes, route_weights, slots, gate_up, down):
    ng = NY * NC
    t_count, width = tokens.shape
    feat = width // ng
    h_local = down.shape[1]
    per_group = nz // 2
    block_rows = per_group * CAP
    group_rows = nx * block_rows
    back_rows = 2 * nx * CAP
    lanes = nz * back_rows

    lane = np.arange(lanes)
    in_plane = lane % back_rows
    entry = in_plane % (nx * CAP)
    lane_info = np.zeros((8, lanes), np.int32)
    lane_info[0] = lane // back_rows * nx + entry // CAP
    lane_info[1] = entry % CAP
    lane_info[2] = in_plane // (nx * CAP)
    r = np.arange(back_rows)
    source = r % (nx * CAP) // CAP * block_rows + r % CAP
    perm_info = np.full((back_rows, 128), -(1 << 20), np.int32)
    perm_info[: nx * CAP, 0] = source[: nx * CAP]
    perm_info[nx * CAP :, 1] = source[nx * CAP :]

    vmem = pl.BlockSpec(memory_space=pltpu.VMEM)
    hbm = pl.BlockSpec(memory_space=pl.ANY)
    smem = pl.BlockSpec(memory_space=pltpu.SMEM)
    mixed, thresholds = pl.pallas_call(
        functools.partial(kernel, nx, nz),
        out_shape=(
            jax.ShapeDtypeStruct((t_count, feat), BF16),
            jax.ShapeDtypeStruct((8, 128), F32),
        ),
        in_specs=[hbm, vmem, vmem, smem, hbm, hbm, vmem, vmem],
        out_specs=(vmem, vmem),
        scratch_shapes=[
            pltpu.VMEM((nz, t_count, feat), BF16),
            pltpu.VMEM((nz, 16, t_count), BF16),
            pltpu.VMEM((2, nx - 1, block_rows, feat), BF16),
            pltpu.VMEM((ng, 2, nx, block_rows, feat), BF16),
            pltpu.VMEM((2 * width, h_local), BF16),
            pltpu.VMEM((ng, feat, 2 * h_local), BF16),
            pltpu.VMEM((ng, h_local, feat), BF16),
            pltpu.VMEM((group_rows, 2 * h_local), F32),
            pltpu.VMEM((ng, 2, group_rows, h_local), BF16),
            pltpu.VMEM((2, nx, block_rows, feat), BF16),
            pltpu.VMEM((2, nx, block_rows, feat), BF16),
            pltpu.VMEM((nz, back_rows, feat // 2), BF16),
            pltpu.VMEM((nz, back_rows, feat // 2), BF16),
            pltpu.VMEM((t_count, lanes), BF16),
            pltpu.VMEM((t_count, lanes), BF16),
            pltpu.VMEM((t_count, feat), F32),
            pltpu.VMEM((128, 768), F32),
            pltpu.VMEM((nx - 1, 8, 128), F32),
            pltpu.VMEM((nx, 8, 128), F32),
            pltpu.VMEM((ng, 8, 128), F32),
            pltpu.VMEM((8, 128), F32),
            pltpu.VMEM((nz, 8, 128), F32),
            pltpu.VMEM((8, 128), F32),
            pltpu.VMEM((nx - 1, 8, 128), F32),
            pltpu.SemaphoreType.DMA((SEMS,)),
            pltpu.SemaphoreType.DMA((SEMS,)),
            pltpu.SemaphoreType.DMA((3,)),
        ],
        compiler_params=pltpu.CompilerParams(
            collective_id=0, has_side_effects=True, vmem_limit_bytes=50 << 20
        ),
        cost_estimate=pl.CostEstimate(flops=4 << 30, bytes_accessed=8 << 20, transcendentals=1 << 17),
    )(
        tokens,
        routes,
        route_weights,
        slots,
        gate_up.reshape(2 * width, h_local),
        down[0],
        jnp.asarray(lane_info),
        jnp.asarray(perm_info),
    )
    return mixed, thresholds[0, : slots.shape[0]]


def solution(mesh, nx=NX, nz=NZ):
    placed = (
        P("ep", None),
        P("ep", None),
        P("ep", None),
        P(),
        P("ep", None, None, "grp"),
        P("ep", "grp", None),
    )
    return jax.shard_map(
        functools.partial(per_device, nx, nz),
        mesh=mesh,
        in_specs=placed,
        out_specs=(P("ep", "grp"), P()),
        check_vma=False,
    )
```

time: 1070 us -> 139 us (0.13)
  the two profiles are of different devices: /device:TPU:32 before, /device:TPU:1 now
where the time goes in v1:
time: 139 us; the launch traced here: 136 us
  Pallas kernels  128 us (92%)
  local copies, waits for them, and re-layouts  7.4 us (5%)
    pallas_call x1, Pallas kernels, per_device(): pl.pallas_call(functools.partial(kernel, nx, nz), out_shape=(jax.ShapeDty...  128 us
    unnamed x13, local copies, waits for them, and re-layouts  6.88 us

profile of v1, /device:TPU:1, one launch (start us, length us, event | category | flops | bytes accessed | tf_op | source)
XLA Modules:
  0.0 136.2 jit_solution(14026696634822300400)
XLA Ops:
  0.6 0.8 copy.10.routes
  1.4 0.8 copy.11.route_weights
  2.2 0.0 copy-start
  2.2 1.2 copy-done
  3.4 0.0 copy-start.1
  3.4 1.2 copy-done.1
  4.7 0.0 copy-start.2
  4.7 0.7 copy-done.2
  5.3 0.0 copy-start.3
  5.3 0.8 copy-done.3
  6.1 0.0 copy-start.4
  6.1 0.8 copy-done.4
  6.9 128.1 %shard_map.95 = (bf16[128,512]{1,0:T(8,128)(2,1)S(1)}, f32[8,128]{1,0:T(8,128)S(1)}) custom-call(bf16[128,4096]{1,0:T(8,128)(2,1)S(1)} %copy-done, s32[128,8]{1,0:T(8,128)S(1)} %copy.10.routes, f32[128,8]{1,0:T(8,128)S(1)} %copy.11.route_weights, s32[64]{0:T(128)S(1)} %copy-done.2, bf16[8192,128]{1,0:T(8,128)(2,1)} %bitcast.5, ...), custom_call_target="tpu_custom_call" | custom-call | flops 4294967296 | bytes 8388608 | tf_op jit(solution)/shard_map/pallas_call | solution.py:607
  135.0 0.5 slice_bitcast_fusion
  135.5 0.7 copy.13
Async XLA Ops:
  2.2 1.2 copy-start
  3.4 1.2 copy-start.1
  4.7 0.7 copy-start.2
  5.3 0.8 copy-start.3
  6.1 0.8 copy-start.4

commit v2 on v0

v2 whole, which is shorter than its diff:
```python
import functools

import jax
import jax.numpy as jnp
from jax import lax
from jax.experimental import pallas as pl
from jax.experimental.pallas import tpu as pltpu
from jax.sharding import PartitionSpec as P

NB = 128
CAP = 10
NY = 4
NC = 2
NX = 4
NZ = 16
NQ = 4
HIST_TOP = 16.0
QUANTILE = 0.999
MESH = pl.DeviceIdType.MESH
F32 = jnp.float32
BF16 = jnp.bfloat16
HIGHEST = lax.Precision.HIGHEST
SEMS = 220
FIRST = 12.0
SPACING = 7.0
AFTER = (0.0, 4.7, 11.0, 15.5, 16.8, 22.0, 23.1, 28.5)


def dot(a, b, precision=None):
    return jnp.dot(a, b, preferred_element_type=F32, precision=precision)


def dot_nt(a, b, precision=None):
    return lax.dot_general(
        a, b, (((1,), (1,)), ((), ())), preferred_element_type=F32, precision=precision
    )


def mask_f32(m):
    return jnp.where(m, 1.0, 0.0)


def mask_bf16(m):
    return mask_f32(m).astype(BF16)


def iota(shape, dim):
    return lax.broadcasted_iota(jnp.int32, shape, dim)


def split(value, by):
    whole = jnp.floor((value + 0.5) * (1.0 / by))
    return whole, value - whole * by


def kernel(
    nx,
    nz,
    tokens,
    routes_t,
    weights_t,
    slots_hbm,
    gate_up,
    down,
    mixed,
    thresholds,
    slots,
    routes_v,
    weights_v,
    own_tokens,
    fwd_send,
    fwd,
    xsend,
    rows,
    w_raw,
    w_split,
    dn,
    acc,
    hid,
    outs,
    outr,
    zsend,
    zrecv,
    perm_in,
    perm_out,
    weights_hi,
    weights_lo,
    total,
    hist,
    plane_send,
    plane_recv,
    valid_send,
    valid_recv,
    count_recv,
    th_send,
    th_recv,
    tx_send,
    tx_recv,
    send_sems,
    recv_sems,
    local_sems,
):
    ng = NY * NC
    planes = nz // NQ
    part_rows = planes * CAP
    quarter_rows = nx * part_rows
    t_count = tokens.shape[0]
    feat = tokens.shape[1] // ng
    half_f = feat // 2
    h_local = down.shape[0]
    picks = routes_t.shape[0]
    back_rows = 2 * nx * CAP

    g = lax.axis_index("grp")
    ep = lax.axis_index("ep")
    y, c = lax.div(g, NC), lax.rem(g, NC)
    x, z = lax.div(ep, nz), lax.rem(ep, nz)
    other = 1 - c

    def g_of(yy, cc):
        return yy * NC + cc

    g_up = g_of(lax.rem(y + 1, NY), c)
    g_dn = g_of(lax.rem(y + NY - 1, NY), c)
    g_op = g_of(lax.rem(y + 2, NY), c)
    g_mate = g_of(y, other)

    def mate_of(q):
        return q + other - c

    offsets = []
    for n in range(NQ - 1):
        offsets += [nz // 2 - 1 - n, n + 1 - nz // 2, n + 1, -1 - n]
    offsets += [nz // 4, -(nz // 4), nz // 2, 0]
    if planes == 1:
        offsets = [1, -1, 2, 0]

    def offset(s):
        return offsets[s]

    def plane(j):
        return lax.rem(z + j + nz, nz)

    def at_z(zz):
        return (g, x * nz + zz)

    def at_x(xx):
        return (g, xx * nz + z)

    def at_g(gg):
        return (gg, ep)

    started = []
    used = [0]

    def send(src, dst, device):
        k = used[0]
        used[0] += 1
        copy = pltpu.make_async_remote_copy(
            src_ref=src,
            dst_ref=dst,
            send_sem=send_sems.at[k],
            recv_sem=recv_sems.at[k],
            device_id=device,
            device_id_type=MESH,
        )
        copy.start()
        started.append(copy)
        return k

    def arrived(k, ref):
        pltpu.make_async_remote_copy(
            src_ref=ref,
            dst_ref=ref,
            send_sem=send_sems.at[k],
            recv_sem=recv_sems.at[k],
            device_id=(g, ep),
            device_id_type=MESH,
        ).wait_recv()

    def take(src, dst, k):
        copy = pltpu.make_async_copy(src, dst, local_sems.at[k])
        copy.start()
        return copy

    mine = pl.ds(pl.multiple_of(g * feat, 128), feat)
    take_routes = take(routes_t, routes_v, 0)
    take_tokens = take(tokens.at[:, mine], own_tokens, 1)
    take_slots = take(slots_hbm, slots, 2)
    take_weights = take(weights_t, weights_v, 3)
    take_w = take(gate_up, w_raw, 4)
    take_down = take(down.at[:, mine], dn.at[g], 5)

    barrier = pltpu.get_barrier_semaphore()
    peers = (
        [at_z(lax.rem(z + j, nz)) for j in range(1, nz)]
        + [at_x(lax.rem(x + i, nx)) for i in range(1, nx)]
        + [at_g(lax.rem(g + q, ng)) for q in range(1, ng)]
    )
    for peer in peers:
        pl.semaphore_signal(barrier, inc=1, device_id=peer, device_id_type=MESH)

    take_routes.wait()
    take_slots.wait()
    routes_f = routes_v[...].astype(F32)
    lines = nz * nx
    experts = jnp.full((lines, 1), -1.0, F32)
    for s in range(nz):
        for i in range(nx):
            e = slots[lax.rem(x + i, nx) * nz + plane(offset(s))].astype(F32)
            experts = jnp.where(iota((lines, 1), 0) == s * nx + i, e, experts)
    chosen = jnp.zeros((lines, t_count), F32)
    for k in range(picks):
        chosen = jnp.where(routes_f[k : k + 1, :] == experts, 1.0, chosen)
    tri = mask_bf16(iota((t_count, t_count), 0) < iota((t_count, t_count), 1))
    earlier = dot(chosen.astype(BF16), tri)
    code = jnp.where(chosen > 0.5, earlier, -100.0)
    number = jnp.sum(chosen, axis=1, keepdims=True)
    for s in range(nz):
        for i in range(nx):
            line = jnp.broadcast_to(number[s * nx + i : s * nx + i + 1, :], (1, 128))
            plane_send[s, i : i + 1, :] = line
        plane_send[s, nx:8, :] = jnp.zeros((8 - nx, 128), F32)

    def pack(value):
        return jnp.concatenate([value[:, :half_f], value[:, half_f:]], axis=0).astype(BF16)

    take_tokens.wait()
    row = iota((nx * CAP, t_count), 0).astype(F32)
    keys = {}

    def dispatch(n):
        sel = []
        for s in range(n * planes, (n + 1) * planes):
            wanted = jnp.zeros((nx * CAP, t_count), F32)
            for i in range(nx):
                place = code[s * nx + i : s * nx + i + 1, :] + float(i * CAP)
                wanted = jnp.where(row == place, 1.0, wanted)
            sel.append(wanted)
        picked = dot(jnp.concatenate(sel, axis=0).astype(BF16), own_tokens[...])
        for k in range(planes):
            s = n * planes + k
            packed = pack(picked[k * nx * CAP : (k + 1) * nx * CAP])
            if offset(s) == 0:
                fwd[s] = packed
            else:
                fwd_send[s] = packed

    def dispatch_send(n):
        for s in range(n * planes, (n + 1) * planes):
            if offset(s):
                to = at_z(plane(offset(s)))
                keys["fwd", s] = send(fwd_send.at[s], fwd.at[s], to)

    dispatch(0)
    pl.semaphore_wait(barrier, len(peers))
    for s in range(nz):
        if offset(s) == 0:
            plane_recv[s] = plane_send[s]
        else:
            keys["plane", s] = send(plane_send.at[s], plane_recv.at[s], at_z(plane(offset(s))))
    dispatch_send(0)
    for n in range(1, NQ):
        dispatch(n)
        dispatch_send(n)
    down_keys = []
    for q in range(1, ng):
        to = lax.rem(g + q, ng)
        columns = pl.ds(pl.multiple_of(to * feat, 128), feat)
        down_keys.append(send(down.at[:, columns], dn.at[g], at_g(to)))

    hist[...] = jnp.zeros_like(hist)

    def swap(a, b):
        row = iota((2 * quarter_rows, 1), 0).astype(F32)
        j, row = split(row, 2 * a * CAP)
        half, row = split(row, a * CAP)
        i, p = split(row, CAP)
        source = i * (2.0 * b * CAP) + half * (b * CAP) + j * CAP + p
        return mask_bf16(iota((2 * quarter_rows, 2 * quarter_rows), 1).astype(F32) == source)

    size = 2 * quarter_rows
    perm_in[...] = swap(planes, nx)
    perm_out[...] = swap(nx, planes)

    def split_weights():
        take_w.wait()
        wide = 2 * 128
        r, q = iota((wide, wide), 0), iota((wide, wide), 1)
        order = mask_bf16(q == jnp.where(r < 128, 2 * r, 2 * (r - 128) + 1))
        per = feat // 128

        @pl.loop(0, ng)
        def _(gg):
            for b in range(per):
                first = pl.multiple_of((gg * per + b) * wide, wide)
                parted = dot(order, w_raw[pl.ds(first, wide)]).astype(BF16)
                half, b = b * 128 // half_f, b * 128 % half_f
                to = 2 * h_local * half
                w_split[gg, b : b + 128, to : to + h_local] = parted[:128]
                w_split[gg, b : b + 128, to + h_local : to + 2 * h_local] = parted[128:]

    def home_weights():
        take_weights.wait()
        eye = mask_f32(iota((t_count, t_count), 0) == iota((t_count, t_count), 1))
        routes_c = dot_nt(eye, routes_v[...].astype(F32), HIGHEST)
        weights_c = dot_nt(eye, weights_v[...], HIGHEST)
        before = mask_bf16(iota((t_count, t_count), 1) < iota((t_count, t_count), 0))
        lane_k, in_plane = split(iota((1, size), 1).astype(F32), back_rows)
        _, entry = split(in_plane, nx * CAP)
        lane_i, place = split(entry, CAP)
        for quarter in range(NQ):
            expert = jnp.full((1, size), -1.0, F32)
            for k in range(planes):
                j = offset(quarter * planes + k)
                for i in range(nx):
                    e = slots[lax.rem(x + i, nx) * nz + plane(j)].astype(F32)
                    expert = jnp.where((lane_k == k) & (lane_i == i), e, expert)
            hit = jnp.zeros((t_count, size), F32)
            weight = hit
            for k in range(picks):
                eq = routes_c[:, k : k + 1] == expert
                hit = jnp.where(eq, 1.0, hit)
                weight = jnp.where(eq, weights_c[:, k : k + 1], weight)
            earlier = dot(before, hit.astype(BF16))
            weight = jnp.where((hit > 0.5) & (earlier == place), weight, 0.0)
            top = weight.astype(BF16)
            weights_hi[quarter] = top
            weights_lo[quarter] = (weight - top.astype(F32)).astype(BF16)

    def select(n):
        for s in range(n * planes, (n + 1) * planes):
            if offset(s):
                arrived(keys["fwd", s], fwd.at[s])
        block = fwd[n * planes : (n + 1) * planes].reshape(size, half_f)
        moved = dot(perm_in[...], block).astype(BF16)
        for i in range(nx):
            part = moved[i * 2 * part_rows : (i + 1) * 2 * part_rows]
            if i == 0:
                rows[g, n, 0] = part
            else:
                xsend[n, i - 1] = part
                keys["x", n, i] = send(
                    xsend.at[n, i - 1], rows.at[g, n, i], at_x(lax.rem(x + i, nx))
                )

    def rows_1(n):
        for i in range(1, nx):
            arrived(keys["x", n, i], rows.at[g, n, i])
        own = rows.at[g, n]
        keys["r_up", n] = send(own, own, at_g(g_up))
        keys["r_dn", n] = send(own, own, at_g(g_dn))
        keys["r_mate", n] = send(own, own, at_g(g_mate))

    near, far = pl.ds(0, nx // 2), pl.ds(nx // 2, nx // 2)

    def rows_2(n):
        ref = rows.at[g_dn, n]
        arrived(keys["r_up", n], ref)
        keys["r_up2", n] = send(rows.at[g_dn, n, near], rows.at[g_dn, n, near], at_g(g_up))
        keys["m_dn", n] = send(ref, ref, at_g(g_mate))
        ref = rows.at[g_up, n]
        arrived(keys["r_dn", n], ref)
        keys["r_dn2", n] = send(rows.at[g_up, n, far], rows.at[g_up, n, far], at_g(g_dn))
        keys["m_up", n] = send(ref, ref, at_g(g_mate))

    def rows_3(n):
        ref = rows.at[g_op, n, near]
        arrived(keys["r_up2", n], ref)
        keys["m_op1", n] = send(ref, ref, at_g(g_mate))
        ref = rows.at[g_op, n, far]
        arrived(keys["r_dn2", n], ref)
        keys["m_op2", n] = send(ref, ref, at_g(g_mate))
        gate_and_up(n, c)

    def rows_4(n):
        arrived(keys["r_mate", n], rows.at[g_mate, n])
        arrived(keys["m_dn", n], rows.at[mate_of(g_dn), n])
        arrived(keys["m_up", n], rows.at[mate_of(g_up), n])
        arrived(keys["m_op1", n], rows.at[mate_of(g_op), n, near])
        arrived(keys["m_op2", n], rows.at[mate_of(g_op), n, far])
        gate_and_up(n, other)
        activate(n)
        own = hid.at[g, n]
        for name, to in (("up", g_up), ("dn", g_dn), ("op", g_op), ("mate", g_mate)):
            keys["h_" + name, n] = send(own, own, at_g(to))
        histogram(n)
        if n == NQ - 1:
            send_counts()

    def hid_2(n):
        for name, src in (("up", g_dn), ("dn", g_up), ("op", g_op)):
            ref = hid.at[src, n]
            arrived(keys["h_" + name, n], ref)
            keys["hm_" + name, n] = send(ref, ref, at_g(g_mate))

    def hid_3(n):
        if n == 0:
            take_down.wait()
            for q in range(1, ng):
                arrived(down_keys[q - 1], dn.at[lax.rem(g + ng - q, ng)])
        arrived(keys["h_mate", n], hid.at[g_mate, n])
        for name, src in (("up", g_dn), ("dn", g_up), ("op", g_op)):
            arrived(keys["hm_" + name, n], hid.at[mate_of(src), n])
        output_rows(n)
        if n == NQ - 1:
            send_threshold()

    def gate_and_up(n, core):
        if n not in begun:
            begun.append(n)
            acc[n] = jnp.zeros((size, 4 * h_local), F32)

        @pl.loop(0, NY)
        def _(yy):
            q = g_of(yy, core)
            acc[n] += dot(rows[q, n].reshape(size, half_f), w_split[q])

    begun = []

    def activate(n):
        both = []
        for i in range(nx):
            r = 2 * part_rows * i
            both.append(
                acc[n, r : r + part_rows, : 2 * h_local]
                + acc[n, r + part_rows : r + 2 * part_rows, 2 * h_local :]
            )
        both = jnp.concatenate(both, axis=0)
        gate = both[:, :h_local]
        hid[g, n] = (gate / (1.0 + jnp.exp(-gate)) * both[:, h_local:]).astype(BF16)

    wide = hist.shape[0] // 8

    def histogram(n):
        @pl.loop(0, quarter_rows // (2 * wide))
        def _(step):
            first = pl.multiple_of(step * 2 * wide, 2 * wide)
            level = jnp.abs(hid[g, n, pl.ds(first, 2 * wide)].astype(F32))
            where = jnp.clip(level * (NB / HIST_TOP) - 0.5, 0.0, NB - 1.0)
            lower = jnp.floor(where)
            part = where - lower
            coarse = jnp.floor(lower * (1.0 / 16.0))
            fine = lower - 16.0 * coarse
            eight = iota((8, h_local), 0).astype(F32)
            sixteen = iota((16, h_local), 0).astype(F32)
            sides = []
            for side in range(2):
                left, one, share = [], [], []
                for r in range(side * wide, (side + 1) * wide):
                    left.append(mask_f32(coarse[r : r + 1] == eight))
                    match = fine[r : r + 1] == sixteen
                    one.append(mask_f32(match))
                    share.append(jnp.where(match, part[r : r + 1], 0.0))
                sides.append(
                    (
                        jnp.concatenate(left, axis=0).astype(BF16),
                        jnp.concatenate(one + share, axis=0).astype(BF16),
                    )
                )
            a = jnp.concatenate([sides[0][0], sides[1][0]], axis=1)
            b = jnp.concatenate([sides[0][1], sides[1][1]], axis=1)
            hist[...] += dot_nt(a, b)

    def counts_of():
        m, k = 8 * wide, 16 * wide
        own_row = lax.shift_right_logical(iota((m, k), 0), 3) == lax.shift_right_logical(
            iota((m, k), 1), 4
        )
        fold = mask_f32((iota((k, NB), 0) & 15) == (iota((k, NB), 1) & 15))
        own_bin = (iota((m, NB), 0) & 7) == lax.shift_right_logical(iota((m, NB), 1), 4)

        def bins(table):
            folded = dot(jnp.where(own_row, table, 0.0), fold, HIGHEST)
            return jnp.sum(jnp.where(own_bin, folded, 0.0), axis=0, keepdims=True)

        number = bins(hist[:, :k])
        share = jnp.broadcast_to(bins(hist[:, k:]), (8, NB))
        return jnp.broadcast_to(number, (8, NB)) - share + pltpu.roll(share, 1, 1)

    def output_rows(n):
        full = jnp.concatenate([hid[q, n] for q in range(ng)], axis=1)
        made = dot(full, dn[...].reshape(ng * h_local, feat))
        for i in range(nx):
            packed = pack(made[i * part_rows : (i + 1) * part_rows])
            if i == 0:
                outr[n, 0] = packed
            else:
                outs[n, i - 1] = packed
                keys["out", n, i] = send(
                    outs.at[n, i - 1], outr.at[n, i], at_x(lax.rem(x + nx - i, nx))
                )

    def z_return(n):
        for i in range(1, nx):
            arrived(keys["out", n, i], outr.at[n, i])
        moved = dot(perm_out[...], outr[n].reshape(size, half_f)).astype(BF16)
        for k in range(planes):
            s = n * planes + k
            block = moved[k * back_rows : (k + 1) * back_rows]
            j = offset(s)
            if j == 0:
                zrecv[s] = block
            else:
                zsend[s] = block
                keys["back", s] = send(zsend.at[s], zrecv.at[s], at_z(plane(-j)))

    def combine(n):
        for s in range(n * planes, (n + 1) * planes):
            if offset(s):
                arrived(keys["back", s], zrecv.at[s])
        back = zrecv[n * planes : (n + 1) * planes].reshape(size, half_f)
        _, in_plane = split(iota((1, size), 1).astype(F32), back_rows)
        upper = in_plane < nx * CAP
        zero = jnp.zeros((), BF16)
        for half in range(2):
            keep = upper if half == 0 else jnp.logical_not(upper)
            high = jnp.where(keep, weights_hi[n], zero)
            low = jnp.where(keep, weights_lo[n], zero)
            gained = dot(high, back) + dot(low, back)
            cols = slice(half * half_f, (half + 1) * half_f)
            if n > 0:
                gained = total[:, cols] + gained
            if n < NQ - 1:
                total[:, cols] = gained
            else:
                mixed[:, cols] = gained.astype(BF16)

    def send_valid():
        number = jnp.zeros((8, 128), F32)
        for s in range(nz):
            if offset(s):
                arrived(keys["plane", s], plane_recv.at[s])
            number = number + plane_recv[s]
        for i in range(nx):
            line = jnp.broadcast_to(number[i : i + 1, :], (8, 128))
            if i == 0:
                valid_recv[0] = line
            else:
                valid_send[i - 1] = line
                keys["valid", i] = send(
                    valid_send.at[i - 1], valid_recv.at[i], at_x(lax.rem(x + i, nx))
                )

    def send_counts():
        counts = counts_of()
        filled = valid_recv[0]
        for i in range(1, nx):
            arrived(keys["valid", i], valid_recv.at[i])
            filled = filled + valid_recv[i]
        empty = (float(NQ * quarter_rows) - filled) * float(h_local)
        count_recv[g] = counts - jnp.where(iota((8, NB), 1) == 0, empty, 0.0)
        for q in range(1, ng):
            keys["count", q] = send(count_recv.at[g], count_recv.at[g], at_g(lax.rem(g + q, ng)))

    def send_threshold():
        for q in range(1, ng):
            arrived(keys["count", q], count_recv.at[lax.rem(g + ng - q, ng)])
        counts = count_recv[0]
        for q in range(1, ng):
            counts = counts + count_recv[q]
        sums = jnp.sum(counts, axis=1, keepdims=True)
        below = mask_f32(iota((NB, NB), 0) < iota((NB, NB), 1))
        before_bin = dot(counts, below, HIGHEST)
        fraction = jnp.clip((QUANTILE * sums - before_bin) / jnp.maximum(counts, 1.0), 0.0, 1.0)
        threshold = (HIST_TOP / NB) * jnp.sum(fraction, axis=1, keepdims=True)
        th_send[...] = jnp.broadcast_to(threshold, (8, 128))
        th_recv[0] = th_send[...]
        for j in range(1, nz):
            keys["th", j] = send(th_send, th_recv.at[j], at_z(plane(j)))

    def share_thresholds():
        gathered = jnp.zeros((8, 128), F32)
        for j in range(nz):
            if j:
                arrived(keys["th", j], th_recv.at[j])
            place = x * nz + plane(-j)
            gathered = jnp.where(iota((8, 128), 1) == place, th_recv[j], gathered)
        tx_send[...] = gathered
        for i in range(1, nx):
            keys["tx", i] = send(tx_send, tx_recv.at[i - 1], at_x(lax.rem(x + i, nx)))

    plan = [(FIRST - 1.0, lambda _: send_valid(), 0)]
    for n in range(NQ):
        for after, step in zip(
            AFTER, (select, rows_1, rows_2, rows_3, rows_4, hid_2, hid_3, z_return), strict=True
        ):
            plan.append((FIRST + SPACING * n + after, step, n))
    split_weights()
    home_weights()
    for _, step, n in sorted(plan, key=lambda entry: entry[0]):
        step(n)

    combine(0)
    combine(1)
    share_thresholds()
    combine(2)
    gathered = tx_send[...]
    for i in range(1, nx):
        arrived(keys["tx", i], tx_recv.at[i - 1])
        gathered = gathered + tx_recv[i - 1]
    thresholds[...] = gathered[0:1, : nx * nz]
    for copy in started:
        copy.wait_send()
    combine(3)


def per_device(nx, nz, tokens, routes, route_weights, slots, gate_up, down):
    ng = NY * NC
    t_count, width = tokens.shape
    picks = routes.shape[1]
    feat = width // ng
    half_f = feat // 2
    h_local = down.shape[1]
    part_rows = nz // NQ * CAP
    quarter_rows = nx * part_rows
    back_rows = 2 * nx * CAP
    size = 2 * quarter_rows
    wide = 16 if quarter_rows % 32 == 0 else 2

    vmem = pl.BlockSpec(memory_space=pltpu.VMEM)
    hbm = pl.BlockSpec(memory_space=pl.ANY)
    mixed, thresholds = pl.pallas_call(
        functools.partial(kernel, nx, nz),
        out_shape=(
            jax.ShapeDtypeStruct((t_count, feat), BF16),
            jax.ShapeDtypeStruct((1, slots.shape[0]), F32),
        ),
        in_specs=[hbm] * 6,
        out_specs=(vmem, vmem),
        scratch_shapes=[
            pltpu.SMEM(slots.shape, jnp.int32),
            pltpu.VMEM((picks, t_count), jnp.int32),
            pltpu.VMEM((picks, t_count), F32),
            pltpu.VMEM((t_count, feat), BF16),
            pltpu.VMEM((nz, back_rows, half_f), BF16),
            pltpu.VMEM((nz, back_rows, half_f), BF16),
            pltpu.VMEM((NQ, nx - 1, 2 * part_rows, half_f), BF16),
            pltpu.VMEM((ng, NQ, nx, 2 * part_rows, half_f), BF16),
            pltpu.VMEM((2 * width, h_local), BF16),
            pltpu.VMEM((ng, half_f, 4 * h_local), BF16),
            pltpu.VMEM((ng, h_local, feat), BF16),
            pltpu.VMEM((NQ, size, 4 * h_local), F32),
            pltpu.VMEM((ng, NQ, quarter_rows, h_local), BF16),
            pltpu.VMEM((NQ, nx - 1, 2 * part_rows, half_f), BF16),
            pltpu.VMEM((NQ, nx, 2 * part_rows, half_f), BF16),
            pltpu.VMEM((nz, back_rows, half_f), BF16),
            pltpu.VMEM((nz, back_rows, half_f), BF16),
            pltpu.VMEM((size, size), BF16),
            pltpu.VMEM((size, size), BF16),
            pltpu.VMEM((NQ, t_count, size), BF16),
            pltpu.VMEM((NQ, t_count, size), BF16),
            pltpu.VMEM((t_count, feat), F32),
            pltpu.VMEM((8 * wide, 32 * wide), F32),
            pltpu.VMEM((nz, 8, 128), F32),
            pltpu.VMEM((nz, 8, 128), F32),
            pltpu.VMEM((nx - 1, 8, 128), F32),
            pltpu.VMEM((nx, 8, 128), F32),
            pltpu.VMEM((ng, 8, 128), F32),
            pltpu.VMEM((8, 128), F32),
            pltpu.VMEM((nz, 8, 128), F32),
            pltpu.VMEM((8, 128), F32),
            pltpu.VMEM((nx - 1, 8, 128), F32),
            pltpu.SemaphoreType.DMA((SEMS,)),
            pltpu.SemaphoreType.DMA((SEMS,)),
            pltpu.SemaphoreType.DMA((6,)),
        ],
        compiler_params=pltpu.CompilerParams(
            collective_id=0, has_side_effects=True, vmem_limit_bytes=60 << 20
        ),
        cost_estimate=pl.CostEstimate(
            flops=4 << 30, bytes_accessed=8 << 20, transcendentals=1 << 17
        ),
    )(
        tokens,
        routes.T,
        route_weights.T,
        slots,
        gate_up.reshape(2 * width, h_local),
        down[0],
    )
    return mixed, thresholds.reshape(-1)


def solution(mesh, nx=NX, nz=NZ):
    placed = (
        P("ep", None),
        P("ep", None),
        P("ep", None),
        P(),
        P("ep", None, None, "grp"),
        P("ep", "grp", None),
    )
    return jax.shard_map(
        functools.partial(per_device, nx, nz),
        mesh=mesh,
        in_specs=placed,
        out_specs=(P("ep", "grp"), P()),
        check_vma=False,
    )
```

time: 1070 us -> 107 us (0.10)
  the two profiles are of different devices: /device:TPU:32 before, /device:TPU:1 now
where the time goes in v2:
time: 107 us
  Pallas kernels  104 us (97%)
  local copies, waits for them, and re-layouts  2.74 us (3%)
    pallas_call x1, Pallas kernels, per_device(): pl.pallas_call(functools.partial(kernel, nx, nz), out_shape=(jax.ShapeDty...  104 us
    unnamed x2, local copies, waits for them, and re-layouts  2.74 us

profile of v2, /device:TPU:1, one launch (start us, length us, event | category | flops | bytes accessed | tf_op | source)
XLA Modules:
  0.0 107.2 jit_solution(5970839056851301624)
XLA Ops:
  0.6 103.8 %shard_map.77 = (bf16[128,512]{1,0:T(8,128)(2,1)}, f32[1,64]{1,0:T(1,128)}) custom-call(bf16[128,4096]{1,0:T(8,128)(2,1)} %tokens.1, s32[8,128]{1,0:T(8,128)} %bitcast.7, f32[8,128]{1,0:T(8,128)} %bitcast.8, s32[64]{0:T(128)} %slots_hbm.1, bf16[8192,128]{1,0:T(8,128)(2,1)} %bitcast.5, bf16[128,4096]{1,0:T(8,128)(2,1)} %bitcast.6), custom_call_target="tpu_custom_call" | custom-call | flops 4294967296 | bytes 8388608 | tf_op jit(solution)/shard_map/pallas_call | solution.py:623
  104.4 1.6 %copy.10 = bf16[128,512]{1,0:T(8,128)(2,1)} copy(bf16[128,512]{1,0:T(8,128)(2,1)} %get-tuple-element.8) | data formatting | bytes 262144
  106.0 1.2 %copy.11 = f32[64]{0:T(128)} copy(f32[64]{0:T(128)} %bitcast.9) | data formatting | bytes 512

commit v3 on v2

--- a/solution.py
+++ b/solution.py
@@ -21,9 +21,11 @@
 BF16 = jnp.bfloat16
 HIGHEST = lax.Precision.HIGHEST
 SEMS = 220
-FIRST = 12.0
-SPACING = 7.0
-AFTER = (0.0, 4.7, 11.0, 15.5, 16.8, 22.0, 23.1, 28.5)
+ORDER = (
+    0, 1, 10, 11, 2, 20, 21, 12, 30, 40, 50, 3,
+    31, 22, 41, 60, 13, 70, 51, 32, 61, 42, 71, 80,
+    23, 52, 62, 81, 72, 33, 43, 53, 82, 63, 73, 83,
+)
 
 
 def dot(a, b, precision=None):
@@ -128,12 +130,7 @@
     def mate_of(q):
         return q + other - c
 
-    offsets = []
-    for n in range(NQ - 1):
-        offsets += [nz // 2 - 1 - n, n + 1 - nz // 2, n + 1, -1 - n]
-    offsets += [nz // 4, -(nz // 4), nz // 2, 0]
-    if planes == 1:
-        offsets = [1, -1, 2, 0]
+    offsets = [8, 0, 2, -2, 1, -1, 5, -5, 3, -3, 7, -7, 4, -4, 6, -6] if nz == 16 else [1, -1, 2, 0]
 
     def offset(s):
         return offsets[s]
@@ -216,12 +213,6 @@
     earlier = dot(chosen.astype(BF16), tri)
     code = jnp.where(chosen > 0.5, earlier, -100.0)
     number = jnp.sum(chosen, axis=1, keepdims=True)
-    for s in range(nz):
-        for i in range(nx):
-            line = jnp.broadcast_to(number[s * nx + i : s * nx + i + 1, :], (1, 128))
-            plane_send[s, i : i + 1, :] = line
-        plane_send[s, nx:8, :] = jnp.zeros((8 - nx, 128), F32)
-
     def pack(value):
         return jnp.concatenate([value[:, :half_f], value[:, half_f:]], axis=0).astype(BF16)
 
@@ -254,21 +245,26 @@
 
     dispatch(0)
     pl.semaphore_wait(barrier, len(peers))
+    down_keys = []
+    for q in range(1, ng):
+        to = lax.rem(g + q, ng)
+        columns = pl.ds(pl.multiple_of(to * feat, 128), feat)
+        down_keys.append(send(down.at[:, columns], dn.at[g], at_g(to)))
+    dispatch_send(0)
+    for n in range(1, NQ):
+        dispatch(n)
+        dispatch_send(n)
+
+    for s in range(nz):
+        for i in range(nx):
+            line = jnp.broadcast_to(number[s * nx + i : s * nx + i + 1, :], (1, 128))
+            plane_send[s, i : i + 1, :] = line
+        plane_send[s, nx:8, :] = jnp.zeros((8 - nx, 128), F32)
     for s in range(nz):
         if offset(s) == 0:
             plane_recv[s] = plane_send[s]
         else:
             keys["plane", s] = send(plane_send.at[s], plane_recv.at[s], at_z(plane(offset(s))))
-    dispatch_send(0)
-    for n in range(1, NQ):
-        dispatch(n)
-        dispatch_send(n)
-    down_keys = []
-    for q in range(1, ng):
-        to = lax.rem(g + q, ng)
-        columns = pl.ds(pl.multiple_of(to * feat, 128), feat)
-        down_keys.append(send(down.at[:, columns], dn.at[g], at_g(to)))
-
     hist[...] = jnp.zeros_like(hist)
 
     def swap(a, b):
@@ -384,9 +380,6 @@
         own = hid.at[g, n]
         for name, to in (("up", g_up), ("dn", g_dn), ("op", g_op), ("mate", g_mate)):
             keys["h_" + name, n] = send(own, own, at_g(to))
-        histogram(n)
-        if n == NQ - 1:
-            send_counts()
 
     def hid_2(n):
         for name, src in (("up", g_dn), ("dn", g_up), ("op", g_op)):
@@ -580,16 +573,15 @@
         for i in range(1, nx):
             keys["tx", i] = send(tx_send, tx_recv.at[i - 1], at_x(lax.rem(x + i, nx)))
 
-    plan = [(FIRST - 1.0, lambda _: send_valid(), 0)]
-    for n in range(NQ):
-        for after, step in zip(
-            AFTER, (select, rows_1, rows_2, rows_3, rows_4, hid_2, hid_3, z_return), strict=True
-        ):
-            plan.append((FIRST + SPACING * n + after, step, n))
+    steps = (select, rows_1, rows_2, rows_3, rows_4, histogram, hid_2, hid_3, z_return)
     split_weights()
     home_weights()
-    for _, step, n in sorted(plan, key=lambda entry: entry[0]):
-        step(n)
+    for entry in ORDER:
+        if entry == 51:
+            send_valid()
+        steps[entry // 10](entry % 10)
+        if entry == 53:
+            send_counts()
 
     combine(0)
     combine(1)

time: 107 us -> 105 us (0.981)
  Pallas kernels: 104 us -> 101 us
    pallas_call x1, Pallas kernels: 104 us -> 101 us  [per_device(): pl.pallas_call(functools.partial(kernel, nx, nz), out_shape=(jax.ShapeDty...]
where the time goes in v3:
time: 105 us; the launch traced here: 104 us
  Pallas kernels  101 us (96%)
  local copies, waits for them, and re-layouts  2.74 us (3%)
    pallas_call x1, Pallas kernels, per_device(): pl.pallas_call(functools.partial(kernel, nx, nz), out_shape=(jax.ShapeDty...  101 us
    unnamed x2, local copies, waits for them, and re-layouts  2.74 us

profile of v3, /device:TPU:1, one launch (start us, length us, event | category | flops | bytes accessed | tf_op | source)
XLA Modules:
  0.0 104.3 jit_solution(16790989018798647163)
XLA Ops:
  0.6 101.0 %shard_map.77 = (bf16[128,512]{1,0:T(8,128)(2,1)}, f32[1,64]{1,0:T(1,128)}) custom-call(bf16[128,4096]{1,0:T(8,128)(2,1)} %tokens.1, s32[8,128]{1,0:T(8,128)} %bitcast.7, f32[8,128]{1,0:T(8,128)} %bitcast.8, s32[64]{0:T(128)} %slots_hbm.1, bf16[8192,128]{1,0:T(8,128)(2,1)} %bitcast.5, bf16[128,4096]{1,0:T(8,128)(2,1)} %bitcast.6), custom_call_target="tpu_custom_call" | custom-call | flops 4294967296 | bytes 8388608 | tf_op jit(solution)/shard_map/pallas_call | solution.py:615
  101.6 1.6 %copy.10 = bf16[128,512]{1,0:T(8,128)(2,1)} copy(bf16[128,512]{1,0:T(8,128)(2,1)} %get-tuple-element.8) | data formatting | bytes 262144
  103.2 1.2 %copy.11 = f32[64]{0:T(128)} copy(f32[64]{0:T(128)} %bitcast.9) | data formatting | bytes 512

commit v4 on v3

--- a/solution.py
+++ b/solution.py
@@ -293,8 +293,9 @@
                 parted = dot(order, w_raw[pl.ds(first, wide)]).astype(BF16)
                 half, b = b * 128 // half_f, b * 128 % half_f
                 to = 2 * h_local * half
-                w_split[gg, b : b + 128, to : to + h_local] = parted[:128]
-                w_split[gg, b : b + 128, to + h_local : to + 2 * h_local] = parted[128:]
+                place = pl.ds(pl.multiple_of(lax.div(gg, NC) * half_f + b, 128), 128)
+                w_split[lax.rem(gg, NC), place, to : to + h_local] = parted[:128]
+                w_split[lax.rem(gg, NC), place, to + h_local : to + 2 * h_local] = parted[128:]
 
     def home_weights():
         take_weights.wait()
@@ -400,14 +401,12 @@
             send_threshold()
 
     def gate_and_up(n, core):
-        if n not in begun:
-            begun.append(n)
-            acc[n] = jnp.zeros((size, 4 * h_local), F32)
-
-        @pl.loop(0, NY)
-        def _(yy):
-            q = g_of(yy, core)
-            acc[n] += dot(rows[q, n].reshape(size, half_f), w_split[q])
+        block = jnp.concatenate(
+            [rows[g_of(yy, core), n].reshape(size, half_f) for yy in range(NY)], axis=1
+        )
+        made = dot(block, w_split[core])
+        acc[n] = acc[n] + made if n in begun else made
+        begun.append(n)
 
     begun = []
 
@@ -630,7 +629,7 @@
             pltpu.VMEM((NQ, nx - 1, 2 * part_rows, half_f), BF16),
             pltpu.VMEM((ng, NQ, nx, 2 * part_rows, half_f), BF16),
             pltpu.VMEM((2 * width, h_local), BF16),
-            pltpu.VMEM((ng, half_f, 4 * h_local), BF16),
+            pltpu.VMEM((NC, NY * half_f, 4 * h_local), BF16),
             pltpu.VMEM((ng, h_local, feat), BF16),
             pltpu.VMEM((NQ, size, 4 * h_local), F32),
             pltpu.VMEM((ng, NQ, quarter_rows, h_local), BF16),

time: 105 us -> 106 us (level)
  Pallas kernels: 101 us -> 103 us
    pallas_call x1, Pallas kernels: 101 us -> 103 us  [per_device(): pl.pallas_call(functools.partial(kernel, nx, nz), out_shape=(jax.ShapeDty...]
where the time goes in v4:
time: 106 us
  Pallas kernels  103 us (97%)
  local copies, waits for them, and re-layouts  2.74 us (3%)
    pallas_call x1, Pallas kernels, per_device(): pl.pallas_call(functools.partial(kernel, nx, nz), out_shape=(jax.ShapeDty...  103 us
    unnamed x2, local copies, waits for them, and re-layouts  2.74 us

profile of v4, /device:TPU:1, one launch (start us, length us, event | category | flops | bytes accessed | tf_op | source)
XLA Modules:
  0.0 106.0 jit_solution(14791524811154145334)
XLA Ops:
  0.6 102.6 %shard_map.77 = (bf16[128,512]{1,0:T(8,128)(2,1)}, f32[1,64]{1,0:T(1,128)}) custom-call(bf16[128,4096]{1,0:T(8,128)(2,1)} %tokens.1, s32[8,128]{1,0:T(8,128)} %bitcast.7, f32[8,128]{1,0:T(8,128)} %bitcast.8, s32[64]{0:T(128)} %slots_hbm.1, bf16[8192,128]{1,0:T(8,128)(2,1)} %bitcast.5, bf16[128,4096]{1,0:T(8,128)(2,1)} %bitcast.6), custom_call_target="tpu_custom_call" | custom-call | flops 4294967296 | bytes 8388608 | tf_op jit(solution)/shard_map/pallas_call | solution.py:614
  103.3 1.6 %copy.10 = bf16[128,512]{1,0:T(8,128)(2,1)} copy(bf16[128,512]{1,0:T(8,128)(2,1)} %get-tuple-element.8) | data formatting | bytes 262144
  104.8 1.2 %copy.11 = f32[64]{0:T(128)} copy(f32[64]{0:T(128)} %bitcast.9) | data formatting | bytes 512
